TPU v7x, 32 devices: a whole 2x2x4 slice. The times are simulated.
32 devices in a mesh: region: 4 (over z), tile: 8 (over y, x, core).
Axes of the slice: x: 2, y: 2, z: 4, core: 2. Of those that a mesh axis runs over, the one named last changes fastest.
Arguments:
- values: bfloat16 [131072, 256], P(('region', 'tile')), may hold values from -6 to 6
- halo_rows: int32 [2, 8192], P(None, ('region', 'tile')), may hold values from 0 to 4095
- neighbors: int32 [6, 131072], P(None, ('region', 'tile')), may hold values from 0 to 4607
- grad_weights: float32 [2, 6, 131072], P(None, None, ('region', 'tile')), may hold values from -2.5 to 2.5
- face_offsets: float32 [2, 6, 131072], P(None, None, ('region', 'tile')), may hold values from -3 to 3
- send_rows: int32 [32, 6144], P(('region', 'tile')), may hold values from 0 to 4095
- margin_slot: int32 [4096, 128], P(('region', 'tile')), may hold values from 0 to 6143, as said below
- margin_cell: int32 [4096, 128], P(('region', 'tile')), may hold values from 0 to 31, as said below
- margin_count: int32 [4096], P(('region', 'tile')), may hold values from 64 to 128, as said below
- margin_area: float32 [4096, 128], P(('region', 'tile')), may hold values from 0.05 to 1
- margin_offset: float32 [2, 4096, 128], P(None, ('region', 'tile')), may hold values from -3 to 3
Outputs:
- target_values: float32 [131072, 256], P(('region', 'tile'))
Inputs may be any that keep to these rules, and one draw needn't show every extreme that they name: `margin_slot`: A tile's margins name rows only from source devices of its own region and of the two neighbouring regions, most of them from its own region. From each such source device only rows below some count are named; every device has some source device with its row 255 named. `margin_cell`: each of a tile's 32 cells is named by one of the tile's first 32 margins. `margin_count`: every device has a tile with all 128 margins live.
All inputs are finite; a program needn't handle non-finite values.
Results may differ from a plain program's by a relative error of at most 0.0011.
Values may be sent and summed in bfloat16 or wider, within the bound.
A program may use at most 64 MiB of HBM per device.

v0:
```python
import math

import jax
import jax.numpy as jnp
from jax import lax
from jax.sharding import PartitionSpec as P

TT = 32


venkat_eps = 0.04


def padded(x, sides, width):
    for axis, dim in sides:
        count, length = (lax.axis_size(axis), x.shape[dim])
        up = [(i, (i + 1) % count) for i in range(count)]
        down = [(j, i) for i, j in up]
        last = lax.slice_in_dim(x, length - width, length, axis=dim)
        initial = lax.slice_in_dim(x, 0, width, axis=dim)
        before = lax.ppermute(last, axis, up)
        after = lax.ppermute(initial, axis, down)
        x = jnp.concatenate([before, x, after], axis=dim)
    return x


def shifted(value, axis, steps):
    count = lax.axis_size(axis)
    pairs = [(source, (source + steps) % count) for source in range(count)]
    return lax.ppermute(value, axis, pairs)


def limited_rows(values_own, extended, neighbor_ids, weighting, face_geom):
    center = values_own.astype(jnp.float32)
    cell_count = center.shape[0]
    stacked = jnp.take(extended, neighbor_ids.reshape(-1), axis=0, mode="clip").reshape(
        6, cell_count, center.shape[1]
    )
    grad_x = jnp.zeros(center.shape, jnp.float32)
    grad_y = jnp.zeros(center.shape, jnp.float32)
    upper_val = center
    lower_val = center
    for face_num in range(6):
        beside = stacked[face_num].astype(jnp.float32)
        difference = beside - center
        grad_x = grad_x + weighting[0, face_num][:, None] * difference
        grad_y = grad_y + weighting[1, face_num][:, None] * difference
        upper_val = jnp.maximum(upper_val, beside)
        lower_val = jnp.minimum(lower_val, beside)
    headroom = upper_val - center
    footroom = center - lower_val
    limiter = jnp.ones(center.shape, jnp.float32)
    for face_num in range(6):
        face_delta = (
            grad_x * face_geom[0, face_num][:, None] + grad_y * face_geom[1, face_num][:, None]
        )
        face_bound = jnp.where(face_delta > 0, headroom, -footroom)
        venkat_ratio = (face_bound * face_bound + venkat_eps + 2.0 * face_delta * face_bound) / (
            face_bound * face_bound
            + 2.0 * face_delta * face_delta
            + face_delta * face_bound
            + venkat_eps
        )
        limiter = jnp.minimum(limiter, venkat_ratio)
    return jnp.concatenate(
        [
            values_own,
            (limiter * grad_x).astype(jnp.bfloat16),
            (limiter * grad_y).astype(jnp.bfloat16),
        ],
        axis=1,
    )


def remap_tiles(arrived, slot_ids, cell_ids, weighting, offset_x, offset_y):
    row_data = (
        jnp.take(arrived, slot_ids.reshape(-1), axis=0, mode="clip")
        .reshape(slot_ids.shape + (arrived.shape[1],))
        .astype(jnp.float32)
    )
    chan_width = row_data.shape[2] // 3
    phi_part = row_data[..., :chan_width]
    slope_x = row_data[..., chan_width : 2 * chan_width]
    slope_y = row_data[..., 2 * chan_width :]
    contribution = weighting[..., None] * (
        phi_part + offset_x[..., None] * slope_x + offset_y[..., None] * slope_y
    )
    one_hot = (cell_ids[:, None, :] == lax.broadcasted_iota(jnp.int32, (1, TT, 1), 1)).astype(
        contribution.dtype
    )
    summed = jnp.einsum("gto,goc->gtc", one_hot, contribution, precision=lax.Precision.HIGHEST)
    area_sum = jnp.einsum("gto,go->gt", one_hot, weighting, precision=lax.Precision.HIGHEST)
    return (summed / area_sum[..., None]).reshape(-1, chan_width)


def local(
    values,
    halo_rows,
    neighbors,
    grad_weights,
    face_offsets,
    send_rows,
    margin_slot,
    margin_cell,
    margin_count,
    margin_area,
    margin_offset,
):
    halo_width = halo_rows.shape[1]
    listed = jnp.take(values, halo_rows.reshape(-1), axis=0, mode="clip")
    widened = padded(listed, ((("region", "tile"), 0),), halo_width)
    extended = jnp.concatenate([values, widened[:halo_width], widened[3 * halo_width :]], axis=0)
    recon = limited_rows(values, extended, neighbors, grad_weights, face_offsets)
    tiles = lax.axis_size("tile")
    rows_each = send_rows.shape[1] // (3 * tiles)
    row_width = recon.shape[1]
    outgoing = jnp.take(recon, send_rows.reshape(-1), axis=0, mode="clip").reshape(
        3, tiles, rows_each, row_width
    )
    within = lax.all_to_all(outgoing, "tile", split_axis=1, concat_axis=1, tiled=True)
    ahead = shifted(within[0], "region", 1)
    behind = shifted(within[2], "region", -1)
    arrived = jnp.stack([ahead, within[1], behind])
    arrived = arrived.reshape(3 * tiles * rows_each, row_width)
    tile_count = margin_slot.shape[0]
    group_size = math.gcd(tile_count, 16)
    is_live = lax.broadcasted_iota(jnp.int32, margin_slot.shape, 1) < margin_count[:, None]
    weight = jnp.where(is_live, margin_area, jnp.zeros_like(margin_area))

    def regroup(block):
        return block.reshape((tile_count // group_size, group_size) + block.shape[1:])

    def one_group(pieces):
        slot_ids, cell_ids, weighting, offset_x, offset_y = pieces
        return remap_tiles(arrived, slot_ids, cell_ids, weighting, offset_x, offset_y)

    mapped = lax.map(
        one_group,
        (
            regroup(margin_slot),
            regroup(margin_cell),
            regroup(weight),
            regroup(margin_offset[0]),
            regroup(margin_offset[1]),
        ),
    )
    return mapped.reshape(tile_count * TT, values.shape[1])


def solution(mesh):
    return jax.shard_map(
        local,
        mesh=mesh,
        in_specs=(
            P(("region", "tile"), None),
            P(None, ("region", "tile")),
            P(None, ("region", "tile")),
            P(None, None, ("region", "tile")),
            P(None, None, ("region", "tile")),
            P(("region", "tile"), None),
            P(("region", "tile"), None),
            P(("region", "tile"), None),
            P(("region", "tile")),
            P(("region", "tile"), None),
            P(None, ("region", "tile"), None),
        ),
        out_specs=P(("region", "tile"), None),
        check_vma=False,
    )
```

profile of v0, /device:TPU:0, one launch (start us, length us, event | category | flops | bytes accessed | tf_op | source)
XLA Modules:
  0.0 590.8 jit_solution(12258857994471790884)
XLA Ops:
  0.7 3.4 gather_fusion.1
  4.7 6.0 %collective-permute-start.1 = (bf16[256,256]{1,0:T(8,128)(2,1)S(1)}, bf16[256,256]{1,0:T(8,128)(2,1)S(1)}, u32[]{:S(2)}, u32[]{:S(2)}) collective-permute-start(bf16[256,256]{1,0:T(8,128)(2,1)S(1)} %get-tuple-element.73), channel_id=1, source_target_pairs={{1,0},{2,1},{3,2},{4,3},{5,4},{6,5},{7,6},{8,7},{9,8},{10,9},{11,1... | collective-permute-start | bytes 393224 | tf_op jit(solution)/shard_map/ppermute | solution.py:22
  10.6 1.2 fusion.61
  11.8 1.2 fusion.62
  13.0 1.0 reshape.104
  14.0 0.7 broadcast_clamp_fusion.1
  14.8 1.7 pad_maximum_fusion.2
  16.5 96.8 %gather_fusion.2 = bf16[24576,256]{1,0:T(8,128)(2,1)} fusion(bf16[4608,256]{1,0:T(8,128)(2,1)S(1)} %pad_maximum_fusion.2, s32[24576]{0:T(1024)S(1)} %broadcast_clamp_fusion), kind=kCustom, calls=%fused_computation.2 | custom fusion | bytes 25264128 | tf_op jit(solution)/shard_map/jit(_take)/gather | solution.py:36
  113.3 27.5 %multiply_convert_fusion.1 = (bf16[4096,256]{1,0:T(8,128)(2,1)S(1)}, f32[4096,256]{1,0:T(8,128)S(1)}, f32[4096,256]{1,0:T(8,128)S(1)}) fusion(f32[4096]{0:T(1024)S(1)} %bitcast.114, f32[4096]{0:T(1024)S(1)} %bitcast.115, f32[4096]{0:T(1024)S(1)} %bitcast.105, f32[4096]{0:T(1024)S(1)} %bitcast.106, f32[4096]{0:T(1024)S(1)} %bitcast.107, ...), kind=kLoop, calls=%fused_computation.97 | loop fusion | flops 161480704 | bytes 25559040 | tf_op jit(solution)/shard_map/convert_element_type | solution.py:68
  140.8 0.8 multiply_convert_fusion
  141.6 0.8 copy-done
  142.4 2.9 pad_maximum_fusion.1
  145.3 31.7 %gather_fusion.3 = bf16[6144,768]{1,0:T(8,128)(2,1)} fusion(bf16[4096,768]{1,0:T(8,128)(2,1)} %pad_maximum_fusion.1, s32[6144]{0:T(1024)S(1)} %broadcast_clamp_fusion.1), kind=kCustom, calls=%fused_computation.3 | custom fusion | bytes 18898944 | tf_op jit(solution)/shard_map/jit(_take)/gather | solution.py:117
  177.0 8.2 %copy.12 = bf16[3,8,256,768]{3,2,0,1:T(8,128)(2,1)} copy(bf16[3,8,256,768]{3,2,1,0:T(8,128)(2,1)} %bitcast.86) | data formatting | bytes 18874368 | tf_op jit(solution)/shard_map/reshape | solution.py:117
  185.2 109.1 %all_to_all.5 = bf16[3,8,256,768]{3,2,0,1:T(8,128)(2,1)S(1)} all-to-all(bf16[3,8,256,768]{3,2,0,1:T(8,128)(2,1)} %copy.12), channel_id=1, replica_groups=mesh['region'=4,'tile'=8] {'tile'}, dimensions={1} | all-to-all | bytes 18874368 | tf_op jit(solution)/shard_map/all_to_all | solution.py:120
  294.3 3.0 slice_bitcast_fusion.2
  297.4 3.7 collective-permute-start.3
  301.2 69.2 %collective-permute-done.2 = bf16[8,256,768]{2,1,0:T(8,128)(2,1)} collective-permute-done((bf16[8,256,768]{2,1,0:T(8,128)(2,1)}, bf16[8,256,768]{2,1,0:T(8,128)(2,1)}, u32[]{:S(2)}, u32[]{:S(2)}) %collective-permute-start.2) | collective-permute-done | bytes 3145760 | tf_op jit(solution)/shard_map/ppermute | solution.py:30
  370.4 63.8 %collective-permute-done.3 = bf16[8,256,768]{2,1,0:T(8,128)(2,1)} collective-permute-done((bf16[8,256,768]{2,1,0:T(8,128)(2,1)}, bf16[8,256,768]{2,1,0:T(8,128)(2,1)}, u32[]{:S(2)}, u32[]{:S(2)}) %collective-permute-start.3) | collective-permute-done | bytes 3145760 | tf_op jit(solution)/shard_map/ppermute | solution.py:30
  434.2 7.0 %pad_maximum_fusion = bf16[3,8,256,768]{3,2,1,0:T(8,128)(2,1)} fusion(bf16[1,8,256,768]{3,2,1,0:T(8,128)(2,1)} %bitcast.44, bf16[1,8,256,768]{3,2,1,0:T(8,128)(2,1)S(1)} %get-tuple-element.71, bf16[1,8,256,768]{3,2,1,0:T(8,128)(2,1)} %bitcast.42), kind=kLoop, calls=%fused_computation.35 | loop fusion | flops 9437184 | bytes 18874368 | tf_op jit(solution)/shard_map/stack | solution.py:123
  441.2 149.6 %while.10 = (s32[]{:T(128)}, f32[8,512,256]{2,1,0:T(8,128)}, s32[8,16,128]{2,1,0:T(8,128)}, f32[8,16,128]{2,1,0:T(8,128)S(1)}, s32[8,16,128]{2,1,0:T(8,128)}, /*...) while((s32[]{:T(128)}, f32[8,512,256]{2,1,0:T(8,128)}, ...), condition=%wide.region_1.2_spmd, body=%wide.region_0.1_spmd.sunk | while | flops 206571520 | bytes 23753328 | solution.py:137
  443.0 13.4 %gather_fusion = bf16[2048,768]{1,0:T(8,128)(2,1)S(1)} fusion(bf16[6144,768]{1,0:T(8,128)(2,1)} %get-tuple-element.176, s32[2048]{0:T(1024)S(1)} %bitcast_clamp_fusion.2), kind=kCustom, calls=%fused_computation.clone.1 | custom fusion | bytes 6299648 | tf_op jit(solution)/shard_map/while/body/eval_jaxpr/jit(_take)/gather | solution.py:77
  457.0 2.1 fusion.75
  459.1 0.8 bitcast_dynamic-update-slice_fusion.2
  461.7 13.4 %gather_fusion = bf16[2048,768]{1,0:T(8,128)(2,1)S(1)} fusion(bf16[6144,768]{1,0:T(8,128)(2,1)} %get-tuple-element.176, s32[2048]{0:T(1024)S(1)} %bitcast_clamp_fusion.2), kind=kCustom, calls=%fused_computation.clone.1 | custom fusion | bytes 6299648 | tf_op jit(solution)/shard_map/while/body/eval_jaxpr/jit(_take)/gather | solution.py:77
  475.7 2.1 fusion.75
  477.8 0.8 bitcast_dynamic-update-slice_fusion.2
  479.7 0.7 bitcast_clamp_fusion.2
  480.4 13.4 %gather_fusion = bf16[2048,768]{1,0:T(8,128)(2,1)S(1)} fusion(bf16[6144,768]{1,0:T(8,128)(2,1)} %get-tuple-element.176, s32[2048]{0:T(1024)S(1)} %bitcast_clamp_fusion.2), kind=kCustom, calls=%fused_computation.clone.1 | custom fusion | bytes 6299648 | tf_op jit(solution)/shard_map/while/body/eval_jaxpr/jit(_take)/gather | solution.py:77
  494.4 2.1 fusion.75
  496.5 0.8 bitcast_dynamic-update-slice_fusion.2
  498.3 0.7 bitcast_clamp_fusion.2
  499.1 13.4 %gather_fusion = bf16[2048,768]{1,0:T(8,128)(2,1)S(1)} fusion(bf16[6144,768]{1,0:T(8,128)(2,1)} %get-tuple-element.176, s32[2048]{0:T(1024)S(1)} %bitcast_clamp_fusion.2), kind=kCustom, calls=%fused_computation.clone.1 | custom fusion | bytes 6299648 | tf_op jit(solution)/shard_map/while/body/eval_jaxpr/jit(_take)/gather | solution.py:77
  513.1 2.1 fusion.75
  515.2 0.8 bitcast_dynamic-update-slice_fusion.2
  517.0 0.7 bitcast_clamp_fusion.2
  517.8 13.4 %gather_fusion = bf16[2048,768]{1,0:T(8,128)(2,1)S(1)} fusion(bf16[6144,768]{1,0:T(8,128)(2,1)} %get-tuple-element.176, s32[2048]{0:T(1024)S(1)} %bitcast_clamp_fusion.2), kind=kCustom, calls=%fused_computation.clone.1 | custom fusion | bytes 6299648 | tf_op jit(solution)/shard_map/while/body/eval_jaxpr/jit(_take)/gather | solution.py:77
  531.8 2.1 fusion.75
  533.9 0.8 bitcast_dynamic-update-slice_fusion.2
  536.5 13.4 %gather_fusion = bf16[2048,768]{1,0:T(8,128)(2,1)S(1)} fusion(bf16[6144,768]{1,0:T(8,128)(2,1)} %get-tuple-element.176, s32[2048]{0:T(1024)S(1)} %bitcast_clamp_fusion.2), kind=kCustom, calls=%fused_computation.clone.1 | custom fusion | bytes 6299648 | tf_op jit(solution)/shard_map/while/body/eval_jaxpr/jit(_take)/gather | solution.py:77
  550.5 2.1 fusion.75
  552.6 0.8 bitcast_dynamic-update-slice_fusion.2
  555.2 13.4 %gather_fusion = bf16[2048,768]{1,0:T(8,128)(2,1)S(1)} fusion(bf16[6144,768]{1,0:T(8,128)(2,1)} %get-tuple-element.176, s32[2048]{0:T(1024)S(1)} %bitcast_clamp_fusion.2), kind=kCustom, calls=%fused_computation.clone.1 | custom fusion | bytes 6299648 | tf_op jit(solution)/shard_map/while/body/eval_jaxpr/jit(_take)/gather | solution.py:77
  569.2 2.1 fusion.75
  571.3 0.8 bitcast_dynamic-update-slice_fusion.2
  573.9 13.4 %gather_fusion = bf16[2048,768]{1,0:T(8,128)(2,1)S(1)} fusion(bf16[6144,768]{1,0:T(8,128)(2,1)} %get-tuple-element.176, s32[2048]{0:T(1024)S(1)} %bitcast_clamp_fusion.2), kind=kCustom, calls=%fused_computation.clone.1 | custom fusion | bytes 6299648 | tf_op jit(solution)/shard_map/while/body/eval_jaxpr/jit(_take)/gather | solution.py:77
  587.9 2.1 fusion.75
  590.0 0.8 bitcast_dynamic-update-slice_fusion.2
  (71 shorter events, 18.6 us)
Async XLA Ops:
  4.1 10.6 %collective-permute-start = (bf16[256,256]{1,0:T(8,128)(2,1)S(1)}, bf16[256,256]{1,0:T(8,128)(2,1)S(1)}, u32[]{:S(2)}, u32[]{:S(2)}) collective-permute-start(bf16[256,256]{1,0:T(8,128)(2,1)S(1)} %get-tuple-element.72), channel_id=1, source_target_pairs={{0,1},{1,2},{2,3},{3,4},{4,5},{5,6},{6,7},{7,8},{8,9},{9,10},{10,1... | collective-permute-start | bytes 393224 | tf_op jit(solution)/shard_map/ppermute | solution.py:21
  4.7 10.1 %collective-permute-start.1 = (bf16[256,256]{1,0:T(8,128)(2,1)S(1)}, bf16[256,256]{1,0:T(8,128)(2,1)S(1)}, u32[]{:S(2)}, u32[]{:S(2)}) collective-permute-start(bf16[256,256]{1,0:T(8,128)(2,1)S(1)} %get-tuple-element.73), channel_id=1, source_target_pairs={{1,0},{2,1},{3,2},{4,3},{5,4},{6,5},{7,6},{8,7},{9,8},{10,9},{11,1... | collective-permute-start | bytes 393224 | tf_op jit(solution)/shard_map/ppermute | solution.py:22
  140.8 1.6 copy-start
  294.3 6.8 %copy-start.2 = (f32[128,128]{1,0:T(8,128)S(1)}, f32[128,128]{1,0:T(8,128)}, u32[]{:S(2)}) copy-start(f32[128,128]{1,0:T(8,128)} %param.22) | copy-start | bytes 196612
  294.3 6.8 %copy-start.3 = (s32[128]{0:T(128)S(1)}, s32[128]{0:T(128)}, u32[]{:S(2)}) copy-start(s32[128]{0:T(128)} %param.21) | copy-start | bytes 1540
  294.3 6.9 %copy-start.1 = (f32[2,128,128]{2,1,0:T(8,128)S(1)}, f32[2,128,128]{2,1,0:T(8,128)}, u32[]{:S(2)}) copy-start(f32[2,128,128]{2,1,0:T(8,128)} %param.23) | copy-start | bytes 393220
  297.3 73.2 %collective-permute-start.2 = (bf16[8,256,768]{2,1,0:T(8,128)(2,1)}, bf16[8,256,768]{2,1,0:T(8,128)(2,1)}, u32[]{:S(2)}, u32[]{:S(2)}) collective-permute-start(bf16[8,256,768]{2,1,0:T(8,128)(2,1)} %get-tuple-element.69), channel_id=1, source_target_pairs={{0,8},{8,16},{16,24},{24,0},{1,9},{9,17},{17,25},{25,1},{2,10},{10... | collective-permute-start | bytes 9437192 | tf_op jit(solution)/shard_map/ppermute | solution.py:30
  297.4 136.8 %collective-permute-start.3 = (bf16[8,256,768]{2,1,0:T(8,128)(2,1)}, bf16[8,256,768]{2,1,0:T(8,128)(2,1)}, u32[]{:S(2)}, u32[]{:S(2)}) collective-permute-start(bf16[8,256,768]{2,1,0:T(8,128)(2,1)} %get-tuple-element.70), channel_id=1, source_target_pairs={{0,24},{8,0},{16,8},{24,16},{1,25},{9,1},{17,9},{25,17},{2,26},{10... | collective-permute-start | bytes 9437192 | tf_op jit(solution)/shard_map/ppermute | solution.py:30
where the time goes:
time: 593 us; the launch traced here: 591 us
  local copies, waits for them, and re-layouts  267 us (45%)
  waiting for transfers between devices  133 us (22%)
  blocking collectives  109 us (18%)
  other arithmetic  51.9 us (9%)
  matrix products  19 us (3%)
  starting transfers between devices  10.3 us (2%)
    ppermute x2, waiting for transfers between devices, shifted(): return lax.ppermute(value, axis, pairs)  133 us
    all_to_all x1, blocking collectives, local(): lax.all_to_all(outgoing, 'tile', split_axis=1, concat_axis=1, tiled=True)  109 us
    gather x8, local copies, waits for them, and re-layouts, remap_tiles(): jnp.take(arrived, slot_ids.reshape(-1), axis=0, mode='clip')  107 us
    gather x1, local copies, waits for them, and re-layouts, limited_rows(): jnp.take(extended, neighbor_ids.reshape(-1), axis=0, mode='clip')  96.8 us
    gather x1, local copies, waits for them, and re-layouts, local(): jnp.take(recon, send_rows.reshape(-1), axis=0, mode='clip')  31.7 us
    convert_element_type x1, other arithmetic, limited_rows(): (limiter * grad_x).astype(jnp.bfloat16)  27.5 us
    dot_general x8, matrix products, remap_tiles(): jnp.einsum('gto,goc->gtc', one_hot, contribution, precision=lax.Precision...  16.6 us
  transfers between devices with their start and end apart: 4, of which 2 were waited for; matrix products, arithmetic and copies ran while one was open for 1% of the time, Pallas kernels for 0%

commit v1 on v0

v1 whole, which is shorter than its diff:
```python
import functools

import jax
import jax.numpy as jnp
from jax import lax
from jax.experimental import pallas as pl
from jax.experimental.pallas import tpu as pltpu
from jax.sharding import PartitionSpec as P

TT = 32
EPS = 0.04
MESH = pl.DeviceIdType.MESH
L = 128
VMEM_LIMIT = 60 * 1024 * 1024


def limit_block(center, beside, geom):
    grad_x = None
    upper = center
    lower = center
    for j in range(6):
        diff = beside[j] - center
        px = geom(j) * diff
        py = geom(6 + j) * diff
        grad_x = px if grad_x is None else grad_x + px
        grad_y = py if j == 0 else grad_y + py
        upper = jnp.maximum(upper, beside[j])
        lower = jnp.minimum(lower, beside[j])
    head = upper - center
    foot = lower - center
    head2 = head * head + EPS
    foot2 = foot * foot + EPS
    num = None
    for j in range(6):
        delta = grad_x * geom(12 + j) + grad_y * geom(18 + j)
        up = delta > 0
        bound = jnp.where(up, head, foot)
        s = jnp.where(up, head2, foot2)
        p = delta * bound
        sp = s + p
        n = sp + p
        d = sp + 2.0 * (delta * delta)
        if num is None:
            less = n < d
            num = jnp.where(less, n, 1.0)
            den = jnp.where(less, d, 1.0)
        else:
            less = n * den < num * d
            num = jnp.where(less, n, num)
            den = jnp.where(less, d, den)
    lim = num / den
    return lim * grad_x, lim * grad_y


def source_kernel(vals, halo, geom, nb, send, out, tab, nbuf, rec, pbuf):
    cells = vals.shape[0]
    extra = halo.shape[0]
    rows = out.shape[0]
    T = 32

    def fill(src, start):
        def body(c, carry):
            b = pl.multiple_of(c * T, T)
            x = src[pl.ds(b, T), :].astype(jnp.float32)
            for h in range(2):
                tab[pl.ds(2 * (start + b) + h, T, stride=2), :] = x[:, h * L : (h + 1) * L]
            return carry

        lax.fori_loop(0, src.shape[0] // T, body, 0)

    fill(vals, 0)
    fill(halo, cells)

    def body(c, carry):
        b = pl.multiple_of(c * T, T)
        for j in range(6):
            for u in range(T):
                i = pl.multiple_of(nb[j * cells + b + u], 2)
                nbuf[pl.ds(2 * (j * T + u), 2), :] = tab[pl.ds(i, 2), :]
        for s in range(T // 8):
            g = geom[pl.ds(b + 8 * s, 8), :]
            cols = [jnp.broadcast_to(g[:, m : m + 1], (8, L)) for m in range(24)]
            for h in range(2):
                center = tab[pl.ds(2 * b + 16 * s + h, 8, stride=2), :]
                beside = [nbuf[pl.ds(2 * (j * T + 8 * s) + h, 8, stride=2), :] for j in range(6)]
                gx, gy = limit_block(center, beside, lambda m: cols[m])
                r = 8 * b + 64 * s
                rec[pl.ds(r + h, 8, stride=8), :] = center
                rec[pl.ds(r + 2 + h, 8, stride=8), :] = gx
                rec[pl.ds(r + 4 + h, 8, stride=8), :] = gy
        return carry

    lax.fori_loop(0, cells // T, body, 0)

    def pack(c, carry):
        b = pl.multiple_of(c * T, T)
        for u in range(T):
            i = pl.multiple_of(send[b + u], 8)
            pbuf[pl.ds(8 * u, 8), :] = rec[pl.ds(i, 8), :]
        for q in range(6):
            out[pl.ds(b, T), q * L : (q + 1) * L] = pbuf[pl.ds(q, T, stride=8), :].astype(jnp.bfloat16)
        return carry

    lax.fori_loop(0, rows // T, pack, 0)


def exchange_kernel(regions, tiles, src, dst, send_sem, recv_sem, own_sem):
    g = lax.axis_index("region")
    k = lax.axis_index("tile")
    rows = src.shape[0] // (3 * tiles)

    barrier = pltpu.get_barrier_semaphore()
    count = 0
    for step in (-1, 0, 1):
        for d in range(tiles):
            if step == 0 and d == 0:
                continue
            where = (lax.rem(g + step + regions, regions), lax.rem(k + d, tiles))
            pl.semaphore_signal(barrier, inc=1, device_id=where, device_id_type=MESH)
            count += 1
    pl.semaphore_wait(barrier, count)

    def block(ref, e, j):
        return ref.at[pl.ds(pl.multiple_of((e * tiles + j) * rows, rows), rows), :]

    sends = []
    for d in range(tiles):
        for e in (0, 2, 1):
            j = lax.rem(k + d, tiles)
            if e == 1 and d == 0:
                continue
            copy = pltpu.make_async_remote_copy(
                src_ref=block(src, e, j),
                dst_ref=block(dst, e, k),
                send_sem=send_sem.at[e * tiles + j],
                recv_sem=recv_sem.at[e * tiles + k],
                device_id=(lax.rem(g + 1 - e + regions, regions), j),
                device_id_type=MESH,
            )
            copy.start()
            sends.append(copy)
    own = pltpu.make_async_copy(block(src, 1, k), block(dst, 1, k), own_sem)
    own.start()
    for d in range(tiles):
        for e in (0, 2, 1):
            j = lax.rem(k + tiles - d, tiles)
            if e == 1 and d == 0:
                continue
            pltpu.make_async_remote_copy(
                src_ref=block(src, e, j),
                dst_ref=block(dst, e, j),
                send_sem=send_sem.at[e * tiles + j],
                recv_sem=recv_sem.at[e * tiles + j],
                device_id=(lax.rem(g + 1 - e + regions, regions), j),
                device_id_type=MESH,
            ).wait_recv()
    for copy in sends:
        copy.wait_send()
    own.wait()


def margin_kernel(arrived, slot, cell, count, area, offset, out, tab, gbuf):
    rows = arrived.shape[0]
    tiles, margins = cell.shape
    T = 32

    def fill(c, carry):
        b = pl.multiple_of(c * T, T)
        for q in range(6):
            tab[pl.ds(8 * b + q, T, stride=8), :] = arrived[pl.ds(b, T), q * L : (q + 1) * L].astype(jnp.float32)
        return carry

    lax.fori_loop(0, rows // T, fill, 0)

    def body(n, carry):
        for u in range(margins):
            i = pl.multiple_of(slot[n * margins + u], 8)
            gbuf[pl.ds(8 * u, 8), :] = tab[pl.ds(i, 8), :]
        one = pl.ds(n, 1)
        lane = lax.broadcasted_iota(jnp.int32, (1, margins), 1)
        w = jnp.where(lane < count[n], area[one, :], 0.0)
        hit = lax.broadcasted_iota(jnp.int32, (TT, margins), 0) == cell[one, :]
        w = jnp.where(hit, w, 0.0)
        total = jnp.sum(w, axis=1, keepdims=True)
        acc = None
        for m, weight in enumerate((w, w * offset[0, one, :], w * offset[1, one, :])):
            high = weight.astype(jnp.bfloat16)
            low = (weight - high.astype(jnp.float32)).astype(jnp.bfloat16)
            lhs = jnp.concatenate([high, low], axis=0)
            rhs = jnp.concatenate(
                [gbuf[pl.ds(2 * m + h, margins, stride=8), :].astype(jnp.bfloat16) for h in range(2)], axis=1
            )
            part = jnp.dot(lhs, rhs, preferred_element_type=jnp.float32)
            acc = part if acc is None else acc + part
        out[pl.ds(pl.multiple_of(n * TT, TT), TT), :] = (acc[:TT] + acc[TT:]) / total
        return carry

    lax.fori_loop(0, tiles, body, 0)


def local(
    values,
    halo_rows,
    neighbors,
    grad_weights,
    face_offsets,
    send_rows,
    margin_slot,
    margin_cell,
    margin_count,
    margin_area,
    margin_offset,
):
    regions = lax.axis_size("region")
    tiles = lax.axis_size("tile")
    devices = regions * tiles
    cells, width = values.shape
    hs = halo_rows.shape[1]
    rows = send_rows.shape[1]
    tile_count, margins = margin_slot.shape
    listed = jnp.take(values, halo_rows.reshape(-1), axis=0, mode="clip")
    axes = ("region", "tile")
    before = lax.ppermute(listed[hs:], axes, [(i, (i + 1) % devices) for i in range(devices)])
    after = lax.ppermute(listed[:hs], axes, [((i + 1) % devices, i) for i in range(devices)])
    halo = jnp.concatenate([before, after], axis=0)
    geom = jnp.concatenate([grad_weights.reshape(12, cells), face_offsets.reshape(12, cells)], axis=0).T
    vmem = pl.BlockSpec(memory_space=pltpu.VMEM)
    smem = pl.BlockSpec(memory_space=pltpu.SMEM)
    hbm = pl.BlockSpec(memory_space=pl.ANY)
    outgoing = pl.pallas_call(
        source_kernel,
        out_shape=jax.ShapeDtypeStruct((rows, 3 * width), jnp.bfloat16),
        in_specs=[vmem, vmem, vmem, smem, smem],
        out_specs=vmem,
        scratch_shapes=[
            pltpu.VMEM((2 * (cells + 2 * hs), L), jnp.float32),
            pltpu.VMEM((2 * 6 * 32, L), jnp.float32),
            pltpu.VMEM((8 * cells, L), jnp.float32),
            pltpu.VMEM((8 * 32, L), jnp.float32),
        ],
        compiler_params=pltpu.CompilerParams(vmem_limit_bytes=VMEM_LIMIT),
        name="source_rows",
    )(values, halo, geom, (neighbors * 2).reshape(-1), (send_rows * 8).reshape(-1))
    arrived = pl.pallas_call(
        functools.partial(exchange_kernel, regions, tiles),
        out_shape=jax.ShapeDtypeStruct((rows, 3 * width), jnp.bfloat16),
        in_specs=[hbm],
        out_specs=hbm,
        scratch_shapes=[
            pltpu.SemaphoreType.DMA((3 * tiles,)),
            pltpu.SemaphoreType.DMA((3 * tiles,)),
            pltpu.SemaphoreType.DMA,
        ],
        compiler_params=pltpu.CompilerParams(collective_id=0, has_side_effects=True, vmem_limit_bytes=VMEM_LIMIT),
        name="exchange_rows",
    )(outgoing)
    return pl.pallas_call(
        margin_kernel,
        out_shape=jax.ShapeDtypeStruct((tile_count * TT, width), jnp.float32),
        in_specs=[vmem, smem, vmem, smem, vmem, vmem],
        out_specs=vmem,
        scratch_shapes=[
            pltpu.VMEM((8 * rows, L), jnp.float32),
            pltpu.VMEM((8 * margins, L), jnp.float32),
        ],
        compiler_params=pltpu.CompilerParams(vmem_limit_bytes=VMEM_LIMIT),
        name="margin_sums",
    )(arrived, (margin_slot * 8).reshape(-1), margin_cell, margin_count, margin_area, margin_offset)


def solution(mesh):
    return jax.shard_map(
        local,
        mesh=mesh,
        in_specs=(
            P(("region", "tile"), None),
            P(None, ("region", "tile")),
            P(None, ("region", "tile")),
            P(None, None, ("region", "tile")),
            P(None, None, ("region", "tile")),
            P(("region", "tile"), None),
            P(("region", "tile"), None),
            P(("region", "tile"), None),
            P(("region", "tile")),
            P(("region", "tile"), None),
            P(None, ("region", "tile"), None),
        ),
        out_specs=P(("region", "tile"), None),
        check_vma=False,
    )
```

time: 593 us -> 257 us (0.43)
  local copies, waits for them, and re-layouts: 267 us -> 8.94 us
  Pallas kernels: 0 us -> 238 us
  waiting for transfers between devices: 133 us -> 0.01 us
  blocking collectives: 109 us -> 0 us
  other arithmetic: 51.9 us -> 2.02 us
  matrix products: 19 us -> 0 us
    pallas_call x0 -> x3, Pallas kernels: none -> 238 us  [the longest x1 140 us: local(): pl.pallas_call(functools.partial(exchange_kernel, regions, tiles), out_sh...]
    gather x10 -> x0, local copies, waits for them, and re-layouts: 235 us -> none  [the longest x8 107 us: remap_tiles(): jnp.take(arrived, slot_ids.reshape(-1), axis=0, mode='clip')]
    ppermute x4 -> x2, waiting for transfers between devices: 133 us -> 0.01 us  [the longest x1 0.01 us: local(): lax.ppermute(listed[hs:], axes, [(i, (i + 1) % devices) for i in range(de...]
    all_to_all x1 -> x0, blocking collectives: 109 us -> none  [local(): lax.all_to_all(outgoing, 'tile', split_axis=1, concat_axis=1, tiled=True)]
    convert_element_type x10 -> x0, other arithmetic: 33.6 us -> none  [the longest x1 27.5 us: limited_rows(): (limiter * grad_x).astype(jnp.bfloat16)]
    dot_general x16 -> x0, matrix products: 19 us -> none  [the longest x8 16.6 us: remap_tiles(): jnp.einsum('gto,goc->gtc', one_hot, contribution, precision=lax.Precision...]
    reshape x1 -> x3, local copies, waits for them, and re-layouts: 8.24 us -> 0.74 us  [the longest x1 0.68 us: local(): (neighbors * 2).reshape(-1)]
    another operation x1 -> x0, other arithmetic: 7.04 us -> none  [local(): arrived = jnp.stack([ahead, within[1], behind])]
  transfers between devices with their start and end apart: 4 -> 2, of which waited for: 2 -> 0; matrix products, arithmetic and copies ran while one was open for 1% -> 2% of each run, Pallas kernels for 0% -> 0%
where the time goes in v1:
time: 257 us; the launch traced here: 256 us
  Pallas kernels  238 us (93%)
  local copies, waits for them, and re-layouts  8.94 us (3%)
  starting transfers between devices  6.49 us (3%)
    pallas_call x1, Pallas kernels, local(): pl.pallas_call(functools.partial(exchange_kernel, regions, tiles), out_sh...  140 us
    pallas_call x1, Pallas kernels, local(): pl.pallas_call(source_kernel, out_shape=jax.ShapeDtypeStruct((rows, 3 * w...  51.9 us
    pallas_call x1, Pallas kernels, local(): pl.pallas_call(margin_kernel, out_shape=jax.ShapeDtypeStruct((tile_count...  46.1 us
    ppermute x1, starting transfers between devices, local(): lax.ppermute(listed[:hs], axes, [((i + 1) % devices, i) for i in range(de...  5.99 us
  transfers between devices with their start and end apart: 2, of which 0 were waited for; matrix products, arithmetic and copies ran while one was open for 2% of the time, Pallas kernels for 0%

profile of v1, /device:TPU:0, one launch (start us, length us, event | category | flops | bytes accessed | tf_op | source)
XLA Modules:
  0.0 255.7 jit_solution(9937530620432165351)
XLA Ops:
  0.0 0.0 copy-start
  0.0 0.0 copy-start.2
  0.0 0.0 copy-start.1
  0.0 0.7 copy.21
  0.7 3.4 %gather_fusion = bf16[512,256]{1,0:T(8,128)(2,1)S(1)} fusion(bf16[4096,256]{1,0:T(8,128)(2,1)} %vals.1, s32[1024]{0:T(1024)S(1)} %pad_clamp_fusion), kind=kCustom, calls=%fused_computation | custom fusion | bytes 526336 | tf_op jit(solution)/shard_map/jit(_take)/gather | solution.py:221
  4.2 0.5 collective-permute-start
  4.7 6.0 %collective-permute-start.1 = (bf16[256,256]{1,0:T(8,128)(2,1)S(1)}, bf16[256,256]{1,0:T(8,128)(2,1)S(1)}, u32[]{:S(2)}, u32[]{:S(2)}) collective-permute-start(bf16[256,256]{1,0:T(8,128)(2,1)S(1)} %get-tuple-element.6), channel_id=1, source_target_pairs={{1,0},{2,1},{3,2},{4,3},{5,4},{6,5},{7,6},{8,7},{9,8},{10,9},{11,1... | collective-permute-start | bytes 393224 | tf_op jit(solution)/shard_map/ppermute | solution.py:224
  10.7 1.0 copy.18
  11.8 1.1 copy.19
  12.9 0.0 copy-done
  12.9 0.0 copy-done.2
  12.9 0.6 broadcast_multiply_fusion.1
  13.6 0.0 copy-done.1
  13.6 0.6 multiply_bitcast_fusion.slot
  14.2 1.9 copy.20
  16.1 0.7 reshape.19.nb
  16.8 0.0 collective-permute-done
  16.8 0.0 collective-permute-done.1
  16.8 0.7 pad_maximum_fusion.1.halo
  17.5 51.9 %source_rows.1.src = bf16[6144,768]{1,0:T(8,128)(2,1)} custom-call(bf16[4096,256]{1,0:T(8,128)(2,1)} %vals.1, bf16[512,256]{1,0:T(8,128)(2,1)} %pad_maximum_fusion.1.halo, f32[4096,24]{1,0:T(8,128)} %bitcast.6, s32[24576]{0:T(1024)} %reshape.19.nb, s32[6144]{0:T(1024)} %bitcast.7), custom_call_target="tpu_custom_call" | custom-call | tf_op jit(solution)/shard_map/source_rows/pallas_call | solution.py:230
  69.4 140.1 %exchange_rows.1.arrived = bf16[6144,768]{1,0:T(8,128)(2,1)} custom-call(bf16[6144,768]{1,0:T(8,128)(2,1)} %source_rows.1.src), custom_call_target="tpu_custom_call" | custom-call | tf_op jit(solution)/shard_map/exchange_rows/pallas_call | solution.py:244
  209.5 46.1 %margin_sums.1 = f32[4096,256]{1,0:T(8,128)} custom-call(bf16[6144,768]{1,0:T(8,128)(2,1)} %exchange_rows.1.arrived, s32[16384]{0:T(1024)} %multiply_bitcast_fusion.slot, s32[128,128]{1,0:T(8,128)} %cell.1, s32[128]{0:T(128)} %count.1, f32[128,128]{1,0:T(8,128)} %area.1, f32[2,128,128]{2,1,0:T(8,128)} %offset.1), custom_call_target="tpu_custom_call" | custom-call | tf_op jit(solution)/shard_map/margin_sums/pallas_call | solution.py:257
  (6 shorter events, 0.1 us)
Async XLA Ops:
  0.0 12.9 %copy-start = (s32[6,4096]{1,0:T(8,128)S(1)}, s32[6,4096]{1,0:T(8,128)}, u32[]{:S(2)}) copy-start(s32[6,4096]{1,0:T(8,128)} %param.13) | copy-start | bytes 294916
  0.0 12.9 %copy-start.2 = (s32[1,6144]{1,0:T(1,128)S(1)}, s32[1,6144]{1,0:T(1,128)}, u32[]{:S(2)}) copy-start(s32[1,6144]{1,0:T(1,128)} %param.16) | copy-start | bytes 73732
  0.0 13.6 %copy-start.1 = (s32[128,128]{1,0:T(8,128)S(1)}, s32[128,128]{1,0:T(8,128)}, u32[]{:S(2)}) copy-start(s32[128,128]{1,0:T(8,128)} %param.17) | copy-start | bytes 196612
  4.2 12.6 %collective-permute-start = (bf16[256,256]{1,0:T(8,128)(2,1)S(1)}, bf16[256,256]{1,0:T(8,128)(2,1)S(1)}, u32[]{:S(2)}, u32[]{:S(2)}) collective-permute-start(bf16[256,256]{1,0:T(8,128)(2,1)S(1)} %get-tuple-element.5), channel_id=1, source_target_pairs={{0,1},{1,2},{2,3},{3,4},{4,5},{5,6},{6,7},{7,8},{8,9},{9,10},{10,1... | collective-permute-start | bytes 393224 | tf_op jit(solution)/shard_map/ppermute | solution.py:223
  4.7 12.1 %collective-permute-start.1 = (bf16[256,256]{1,0:T(8,128)(2,1)S(1)}, bf16[256,256]{1,0:T(8,128)(2,1)S(1)}, u32[]{:S(2)}, u32[]{:S(2)}) collective-permute-start(bf16[256,256]{1,0:T(8,128)(2,1)S(1)} %get-tuple-element.6), channel_id=1, source_target_pairs={{1,0},{2,1},{3,2},{4,3},{5,4},{6,5},{7,6},{8,7},{9,8},{10,9},{11,1... | collective-permute-start | bytes 393224 | tf_op jit(solution)/shard_map/ppermute | solution.py:224

commit v2 on v1

v2 whole, which is shorter than its diff:
```python
import functools

import jax
import jax.numpy as jnp
from jax import lax
from jax.experimental import pallas as pl
from jax.experimental.pallas import tpu as pltpu
from jax.sharding import PartitionSpec as P

TT = 32
EPS = 0.04
MESH = pl.DeviceIdType.MESH
L = 128
VMEM_LIMIT = 60 * 1024 * 1024


def limit_block(center, beside, geom):
    grad_x = None
    upper = center
    lower = center
    for j in range(6):
        diff = beside[j] - center
        px = geom(j) * diff
        py = geom(6 + j) * diff
        grad_x = px if grad_x is None else grad_x + px
        grad_y = py if j == 0 else grad_y + py
        upper = jnp.maximum(upper, beside[j])
        lower = jnp.minimum(lower, beside[j])
    head = upper - center
    foot = lower - center
    head2 = head * head + EPS
    foot2 = foot * foot + EPS
    num = None
    for j in range(6):
        delta = grad_x * geom(12 + j) + grad_y * geom(18 + j)
        up = delta > 0
        bound = jnp.where(up, head, foot)
        s = jnp.where(up, head2, foot2)
        p = delta * bound
        sp = s + p
        n = sp + p
        d = sp + 2.0 * (delta * delta)
        if num is None:
            less = n < d
            num = jnp.where(less, n, 1.0)
            den = jnp.where(less, d, 1.0)
        else:
            less = n * den < num * d
            num = jnp.where(less, n, num)
            den = jnp.where(less, d, den)
    lim = num / den
    return lim * grad_x, lim * grad_y


def loop(count, body):
    def step(c, carry):
        body(c)
        return carry

    lax.fori_loop(0, count, step, 0)


def unrolled(count, body):
    def step(c, carry):
        body(c)
        return carry

    lax.fori_loop(0, count, step, 0, unroll=True)


def remap_kernel(
    regions, tiles, vals, geom, nb, send, listed, slot, cell, count, area, offset, out,
    tab, nbuf, rec, pbuf, hsend, hrecv, s0, s1, s2, r0, r1, r2, mtab, gbuf,
    hsend_sem, hrecv_sem, send_sem, recv_sem,
):
    g = lax.axis_index("region")
    k = lax.axis_index("tile")
    devices = regions * tiles
    me = g * tiles + k
    cells = vals.shape[0]
    hs = hsend.shape[0] // 2
    rows = s0.shape[0] // (3 * tiles)
    tile_count, margins = cell.shape
    T = 32

    barrier = pltpu.get_barrier_semaphore()
    partners = 0
    for step in (-1, 0, 1):
        for d in range(tiles):
            if step == 0 and d == 0:
                continue
            where = (lax.rem(g + step + regions, regions), lax.rem(k + d, tiles))
            pl.semaphore_signal(barrier, inc=1, device_id=where, device_id_type=MESH)
            partners += 1

    def fill(src, start):
        def body(c):
            b = pl.multiple_of(c * T, T)
            x = src[pl.ds(b, T), :].astype(jnp.float32)
            for h in range(2):
                pbuf[pl.ds(h, T, stride=2), :] = x[:, h * L : (h + 1) * L]

            def one(u):
                tab[start + b + u] = pbuf[pl.ds(2 * u, 2), :]

            unrolled(T, one)

        loop(src.shape[0] // T, body)

    fill(vals, 0)
    pl.semaphore_wait(barrier, partners)

    def pack_values(index, src_row, dst, dst_row, n):
        def body(c):
            b = pl.multiple_of(c * T, T)

            def one(u):
                pbuf[pl.ds(2 * u, 2), :] = tab[index[src_row + b + u]]

            unrolled(T, one)
            at = pl.ds(pl.multiple_of(dst_row + b, T), T)
            for h in range(2):
                dst[at, h * L : (h + 1) * L] = pbuf[pl.ds(h, T, stride=2), :].astype(jnp.bfloat16)

        loop(n // T, body)

    pack_values(listed, 0, hsend, 0, 2 * hs)
    halo = []
    for part, step in ((1, 1), (0, devices - 1)):
        to = lax.rem(me + step, devices)
        copy = pltpu.make_async_remote_copy(
            src_ref=hsend.at[pl.ds(part * hs, hs), :],
            dst_ref=hrecv.at[pl.ds((1 - part) * hs, hs), :],
            send_sem=hsend_sem.at[part],
            recv_sem=hrecv_sem.at[part],
            device_id=(to // tiles, lax.rem(to, tiles)),
            device_id_type=MESH,
        )
        copy.start()
        halo.append(copy)

    def block_row(e, j):
        return pl.multiple_of((e * tiles + j) * rows, rows)

    def remote(p, src, dst, e, j, at):
        return pltpu.make_async_remote_copy(
            src_ref=src.at[pl.ds(block_row(e, j), rows), :],
            dst_ref=dst.at[pl.ds(block_row(e, at), rows), :],
            send_sem=send_sem.at[p * 3 * tiles + e * tiles + j],
            recv_sem=recv_sem.at[p * 3 * tiles + e * tiles + at],
            device_id=(lax.rem(g + 1 - e + regions, regions), j),
            device_id_type=MESH,
        )

    def each_block(body):
        def far(d):
            j = lax.rem(k + d, tiles)
            body(0, j)
            body(2, j)

        loop(tiles, far)
        loop(tiles - 1, lambda d: body(1, lax.rem(k + d + 1, tiles)))

    def receive(p, src, dst):
        def far(d):
            j = lax.rem(k + d, tiles)
            remote(p, src, dst, 0, j, j).wait_recv()
            remote(p, src, dst, 2, j, j).wait_recv()

        def near(d):
            j = lax.rem(k + d + 1, tiles)
            remote(p, src, dst, 1, j, j).wait_recv()

        loop(tiles, far)
        loop(tiles - 1, near)

    def send_values(e, j):
        row = block_row(e, j)
        pack_values(send, row, s0, row, rows)
        remote(0, s0, r0, e, j, k).start()

    each_block(send_values)
    pack_values(send, block_row(1, k), r0, block_row(1, k), rows)

    for copy in halo:
        copy.wait_recv()
    fill(hrecv, cells)

    def source(c):
        b = pl.multiple_of(c * T, T)
        for j in range(6):

            def one(u):
                nbuf[pl.ds(2 * (j * T + u), 2), :] = tab[nb[j * cells + b + u]]

            unrolled(T, one)
        mine = vals[pl.ds(b, T), :].astype(jnp.float32)
        for s in range(T // 8):
            w = geom[pl.ds(b + 8 * s, 8), :]
            cols = [jnp.broadcast_to(w[:, m : m + 1], (8, L)) for m in range(24)]
            for h in range(2):
                center = mine[8 * s : 8 * s + 8, h * L : (h + 1) * L]
                beside = [nbuf[pl.ds(2 * (j * T + 8 * s) + h, 8, stride=2), :] for j in range(6)]
                gx, gy = limit_block(center, beside, lambda m: cols[m])
                pbuf[pl.ds(32 * s + h, 8, stride=4), :] = gx
                pbuf[pl.ds(32 * s + 2 + h, 8, stride=4), :] = gy

        def keep(u):
            rec[b + u] = pbuf[pl.ds(4 * u, 4), :]

        unrolled(T, keep)

    loop(cells // T, source)

    def pack_slopes(src_row, to1, to2):
        def body(c):
            b = pl.multiple_of(c * T, T)

            def one(u):
                pbuf[pl.ds(4 * u, 4), :] = rec[send[src_row + b + u]]

            unrolled(T, one)
            at = pl.ds(pl.multiple_of(src_row + b, T), T)
            for h, dst in enumerate((to1, to2)):
                for m in range(2):
                    dst[at, m * L : (m + 1) * L] = pbuf[pl.ds(2 * m + h, T, stride=4), :].astype(jnp.bfloat16)

        loop(rows // T, body)

    def send_slopes(e, j):
        pack_slopes(block_row(e, j), s1, s2)
        remote(1, s1, r1, e, j, k).start()

    each_block(send_slopes)
    pack_slopes(block_row(1, k), r1, r2)

    def margin(p, arrived):
        def spread(c):
            b = pl.multiple_of(c * T, T)
            x = arrived[pl.ds(b, T), :].astype(jnp.float32)
            for h in range(2):
                pbuf[pl.ds(h, T, stride=2), :] = x[:, h * L : (h + 1) * L]

            def one(u):
                mtab[b + u] = pbuf[pl.ds(2 * u, 2), :]

            unrolled(T, one)

        loop(arrived.shape[0] // T, spread)

        def split(weight):
            high = weight.astype(jnp.bfloat16)
            low = (weight - high.astype(jnp.float32)).astype(jnp.bfloat16)
            return jnp.concatenate([high, low], axis=0)

        def body(n):
            def one(u):
                gbuf[pl.ds(2 * u, 2), :] = mtab[slot[n * margins + u]]

            unrolled(margins, one)
            tile = pl.ds(n, 1)
            lane = lax.broadcasted_iota(jnp.int32, (1, margins), 1)
            w = jnp.where(lane < count[n], area[tile, :], 0.0)
            hit = lax.broadcasted_iota(jnp.int32, (TT, margins), 0) == cell[tile, :]
            w = jnp.where(hit, w, 0.0)
            total = jnp.sum(w, axis=1, keepdims=True)
            parts = [gbuf[pl.ds(h, margins, stride=2), :].astype(jnp.bfloat16) for h in range(2)]
            at = pl.ds(pl.multiple_of(n * TT, TT), TT)
            if p == 0:
                acc = jnp.dot(split(w), jnp.concatenate(parts, axis=1), preferred_element_type=jnp.float32)
                out[at, :] = (acc[:TT] + acc[TT:]) / total
            else:
                lhs = jnp.concatenate([split(w * offset[0, tile, :]), split(w * offset[1, tile, :])], axis=1)
                acc = jnp.dot(lhs, jnp.concatenate(parts, axis=0), preferred_element_type=jnp.float32)
                lanes = slice((p - 1) * L, p * L)
                out[at, lanes] = out[at, lanes] + (acc[:TT] + acc[TT:]) / total

        loop(tile_count, body)

    receive(0, s0, r0)
    margin(0, r0)
    each_block(lambda e, j: remote(2, s2, r2, e, j, k).start())
    receive(1, s1, r1)
    margin(1, r1)
    receive(2, s2, r2)
    margin(2, r2)
    for copy in halo:
        copy.wait_send()
    for p, src, dst in ((0, s0, r0), (1, s1, r1), (2, s2, r2)):
        each_block(lambda e, j: remote(p, src, dst, e, j, k).wait_send())


def local(
    values,
    halo_rows,
    neighbors,
    grad_weights,
    face_offsets,
    send_rows,
    margin_slot,
    margin_cell,
    margin_count,
    margin_area,
    margin_offset,
):
    regions = lax.axis_size("region")
    tiles = lax.axis_size("tile")
    cells, width = values.shape
    hs = halo_rows.shape[1]
    rows = send_rows.shape[1]
    tile_count, margins = margin_slot.shape
    geom = jnp.concatenate([grad_weights.reshape(12, cells), face_offsets.reshape(12, cells)], axis=0).T
    vmem = pl.BlockSpec(memory_space=pltpu.VMEM)
    smem = pl.BlockSpec(memory_space=pltpu.SMEM)
    block = pltpu.VMEM((rows, width), jnp.bfloat16)
    halo = pltpu.VMEM((2 * hs, width), jnp.bfloat16)
    return pl.pallas_call(
        functools.partial(remap_kernel, regions, tiles),
        out_shape=jax.ShapeDtypeStruct((tile_count * TT, width), jnp.float32),
        in_specs=[vmem, vmem, smem, smem, smem, smem, vmem, smem, vmem, vmem],
        out_specs=vmem,
        scratch_shapes=[
            pltpu.VMEM((cells + 2 * hs, 2, L), jnp.float32),
            pltpu.VMEM((2 * 6 * 32, L), jnp.float32),
            pltpu.VMEM((cells, 4, L), jnp.float32),
            pltpu.VMEM((4 * 32, L), jnp.float32),
            halo,
            halo,
            block,
            block,
            block,
            block,
            block,
            block,
            pltpu.VMEM((rows, 2, L), jnp.float32),
            pltpu.VMEM((2 * margins, L), jnp.float32),
            pltpu.SemaphoreType.DMA((2,)),
            pltpu.SemaphoreType.DMA((2,)),
            pltpu.SemaphoreType.DMA((9 * tiles,)),
            pltpu.SemaphoreType.DMA((9 * tiles,)),
        ],
        compiler_params=pltpu.CompilerParams(collective_id=0, has_side_effects=True, vmem_limit_bytes=VMEM_LIMIT),
        name="remap",
    )(
        values,
        geom,
        neighbors.reshape(-1),
        send_rows.reshape(-1),
        halo_rows.reshape(-1),
        margin_slot.reshape(-1),
        margin_cell,
        margin_count,
        margin_area,
        margin_offset,
    )


def solution(mesh):
    return jax.shard_map(
        local,
        mesh=mesh,
        in_specs=(
            P(("region", "tile"), None),
            P(None, ("region", "tile")),
            P(None, ("region", "tile")),
            P(None, None, ("region", "tile")),
            P(None, None, ("region", "tile")),
            P(("region", "tile"), None),
            P(("region", "tile"), None),
            P(("region", "tile"), None),
            P(("region", "tile")),
            P(("region", "tile"), None),
            P(None, ("region", "tile"), None),
        ),
        out_specs=P(("region", "tile"), None),
        check_vma=False,
    )
```

time: 257 us -> 210 us (0.82)
  Pallas kernels: 238 us -> 196 us
  starting transfers between devices: 6.49 us -> 0 us
    pallas_call x3 -> x1, Pallas kernels: 238 us -> 196 us  [local(): pl.pallas_call(functools.partial(remap_kernel, regions, tiles), out_shape...]
    ppermute x2 -> x0, starting transfers between devices: 6.49 us -> none  [the longest x1 5.99 us: local(): lax.ppermute(listed[:hs], axes, [((i + 1) % devices, i) for i in range(de...]
    unnamed x9 -> x4, local copies, waits for them, and re-layouts: 2.83 us -> 7.82 us
    gather x1 -> x0, local copies, waits for them, and re-layouts: 3.42 us -> none  [local(): listed = jnp.take(values, halo_rows.reshape(-1), axis=0, mode='clip')]
  transfers between devices with their start and end apart: 2 -> 0, of which waited for: 0 -> 0; matrix products, arithmetic and copies ran while one was open for 2% -> 0% of each run, Pallas kernels for 0% -> 0%
where the time goes in v2:
time: 210 us; the launch traced here: 208 us
  Pallas kernels  196 us (93%)
  local copies, waits for them, and re-layouts  11.4 us (5%)
    pallas_call x1, Pallas kernels, local(): pl.pallas_call(functools.partial(remap_kernel, regions, tiles), out_shape...  196 us
    unnamed x4, local copies, waits for them, and re-layouts  7.82 us

profile of v2, /device:TPU:0, one launch (start us, length us, event | category | flops | bytes accessed | tf_op | source)
XLA Modules:
  0.0 207.5 jit_solution(644149644334527408)
XLA Ops:
  0.0 1.2 copy.21
  1.2 1.6 reshape.20.nb
  2.8 1.0 copy.18
  3.9 1.1 copy.19
  5.1 1.9 copy.20
  7.0 196.0 %remap.1 = f32[4096,256]{1,0:T(8,128)} custom-call(bf16[4096,256]{1,0:T(8,128)(2,1)} %vals.1, f32[4096,24]{1,0:T(8,128)} %bitcast.5, s32[24576]{0:T(1024)} %reshape.20.nb, s32[6144]{0:T(1024)} %bitcast.7, s32[512]{0:T(512)} %bitcast.8, s32[16384]{0:T(1024)} %bitcast.6, s32[128,128]{1,0:T(8,128)} %cell.1, s32[128]{0:T(128)} %count.1, f32[128,128]{1,0:T(8,128)} %area.1, ...), custom_call_target="tpu_custom_call" | custom-call | tf_op jit(solution)/shard_map/remap/pallas_call | solution.py:317
  203.1 4.5 %copy.23 = f32[4096,256]{1,0:T(8,128)} copy(f32[4096,256]{1,0:T(8,128)} %remap.1) | data formatting | bytes 8388608
  (3 shorter events, 0.1 us)

commit v3 on v2

--- a/solution.py
+++ b/solution.py
@@ -69,8 +69,8 @@
 
 
 def remap_kernel(
-    regions, tiles, vals, geom, nb, send, listed, slot, cell, count, area, offset, out,
-    tab, nbuf, rec, pbuf, hsend, hrecv, s0, s1, s2, r0, r1, r2, mtab, gbuf,
+    regions, tiles, vals, weights, faces, nb, send, listed, slot, cell, count, area, offset, out,
+    tab, nbuf, rec, pbuf, hsend, hrecv, s0, s1, s2, r0, r1, r2, mtab, gbuf, gstack, geom,
     hsend_sem, hrecv_sem, send_sem, recv_sem,
 ):
     g = lax.axis_index("region")
@@ -82,6 +82,8 @@
     rows = s0.shape[0] // (3 * tiles)
     tile_count, margins = cell.shape
     T = 32
+    C = 128
+    G = gbuf.shape[0] // (2 * margins)
 
     barrier = pltpu.get_barrier_semaphore()
     partners = 0
@@ -93,38 +95,40 @@
             pl.semaphore_signal(barrier, inc=1, device_id=where, device_id_type=MESH)
             partners += 1
 
+    def spread(src, b, dst, start):
+        for v in range(0, C, T):
+            x = src[pl.ds(b + v, T), :].astype(jnp.float32)
+            for h in range(2):
+                pbuf[pl.ds(2 * v + h, T, stride=2), :] = x[:, h * L : (h + 1) * L]
+
+            def one(u):
+                dst[start + b + v + u] = pbuf[pl.ds(2 * (v + u), 2), :]
+
+            unrolled(T, one)
+
     def fill(src, start):
-        def body(c):
-            b = pl.multiple_of(c * T, T)
-            x = src[pl.ds(b, T), :].astype(jnp.float32)
-            for h in range(2):
-                pbuf[pl.ds(h, T, stride=2), :] = x[:, h * L : (h + 1) * L]
-
-            def one(u):
-                tab[start + b + u] = pbuf[pl.ds(2 * u, 2), :]
-
-            unrolled(T, one)
-
-        loop(src.shape[0] // T, body)
+        loop(src.shape[0] // C, lambda c: spread(src, pl.multiple_of(c * C, C), tab, start))
 
     fill(vals, 0)
     pl.semaphore_wait(barrier, partners)
 
     def pack_values(index, src_row, dst, dst_row, n):
         def body(c):
-            b = pl.multiple_of(c * T, T)
-
-            def one(u):
-                pbuf[pl.ds(2 * u, 2), :] = tab[index[src_row + b + u]]
-
-            unrolled(T, one)
-            at = pl.ds(pl.multiple_of(dst_row + b, T), T)
-            for h in range(2):
-                dst[at, h * L : (h + 1) * L] = pbuf[pl.ds(h, T, stride=2), :].astype(jnp.bfloat16)
-
-        loop(n // T, body)
-
-    pack_values(listed, 0, hsend, 0, 2 * hs)
+            b = pl.multiple_of(c * C, C)
+            for v in range(0, C, T):
+
+                def one(u):
+                    pbuf[pl.ds(2 * (v + u), 2), :] = tab[index(src_row + b + v + u)]
+
+                unrolled(T, one)
+                at = pl.ds(pl.multiple_of(dst_row + b, C) + v, T)
+                for h in range(2):
+                    dst[at, h * L : (h + 1) * L] = pbuf[pl.ds(2 * v + h, T, stride=2), :].astype(jnp.bfloat16)
+
+        loop(n // C, body)
+
+    for part in range(2):
+        pack_values(lambda r: listed[part, r], 0, hsend, part * hs, hs)
     halo = []
     for part, step in ((1, 1), (0, devices - 1)):
         to = lax.rem(me + step, devices)
@@ -176,56 +180,69 @@
 
     def send_values(e, j):
         row = block_row(e, j)
-        pack_values(send, row, s0, row, rows)
+        pack_values(lambda r: send[0, r], row, s0, row, rows)
         remote(0, s0, r0, e, j, k).start()
 
     each_block(send_values)
-    pack_values(send, block_row(1, k), r0, block_row(1, k), rows)
+    pack_values(lambda r: send[0, r], block_row(1, k), r0, block_row(1, k), rows)
 
     for copy in halo:
         copy.wait_recv()
     fill(hrecv, cells)
 
-    def source(c):
-        b = pl.multiple_of(c * T, T)
-        for j in range(6):
-
-            def one(u):
-                nbuf[pl.ds(2 * (j * T + u), 2), :] = tab[nb[j * cells + b + u]]
-
-            unrolled(T, one)
-        mine = vals[pl.ds(b, T), :].astype(jnp.float32)
-        for s in range(T // 8):
-            w = geom[pl.ds(b + 8 * s, 8), :]
-            cols = [jnp.broadcast_to(w[:, m : m + 1], (8, L)) for m in range(24)]
-            for h in range(2):
-                center = mine[8 * s : 8 * s + 8, h * L : (h + 1) * L]
-                beside = [nbuf[pl.ds(2 * (j * T + 8 * s) + h, 8, stride=2), :] for j in range(6)]
-                gx, gy = limit_block(center, beside, lambda m: cols[m])
-                pbuf[pl.ds(32 * s + h, 8, stride=4), :] = gx
-                pbuf[pl.ds(32 * s + 2 + h, 8, stride=4), :] = gy
-
-        def keep(u):
-            rec[b + u] = pbuf[pl.ds(4 * u, 4), :]
-
-        unrolled(T, keep)
-
-    loop(cells // T, source)
+    gstack[...] = jnp.zeros_like(gstack)
+
+    def source_chunk(o):
+        chunk = pl.multiple_of(o * C, C)
+        for m in range(2):
+            gstack[8 * m : 8 * m + 6, :] = weights[m, :, pl.ds(chunk, C)]
+            gstack[16 + 8 * m : 22 + 8 * m, :] = faces[m, :, pl.ds(chunk, C)]
+        geom[...] = gstack[...].T
+
+        def source(c):
+            t = pl.multiple_of(c * T, T)
+            b = pl.multiple_of(chunk + t, T)
+            mine = vals[pl.ds(b, T), :].astype(jnp.float32)
+            for s in range(T // 8):
+
+                def gather(q):
+                    j = q // 8
+                    u = 8 * s + q % 8
+                    nbuf[pl.ds(2 * (48 * s + q), 2), :] = tab[nb[j, b + u]]
+
+                for q in range(48):
+                    gather(q)
+                w = geom[pl.ds(t + 8 * s, 8), :]
+                cols = [jnp.broadcast_to(w[:, m : m + 1], (8, L)) for m in range(32)]
+                for h in range(2):
+                    center = mine[8 * s : 8 * s + 8, h * L : (h + 1) * L]
+                    beside = [nbuf[pl.ds(2 * (48 * s + 8 * j) + h, 8, stride=2), :] for j in range(6)]
+                    gx, gy = limit_block(center, beside, lambda m: cols[m + 2 * (m // 6)])
+                    pbuf[pl.ds(32 * s + h, 8, stride=4), :] = gx
+                    pbuf[pl.ds(32 * s + 2 + h, 8, stride=4), :] = gy
+                for u in range(8 * s, 8 * s + 8):
+                    rec[b + u] = pbuf[pl.ds(4 * u, 4), :]
+
+        loop(C // T, source)
+
+    loop(cells // C, source_chunk)
 
     def pack_slopes(src_row, to1, to2):
         def body(c):
-            b = pl.multiple_of(c * T, T)
-
-            def one(u):
-                pbuf[pl.ds(4 * u, 4), :] = rec[send[src_row + b + u]]
-
-            unrolled(T, one)
-            at = pl.ds(pl.multiple_of(src_row + b, T), T)
-            for h, dst in enumerate((to1, to2)):
-                for m in range(2):
-                    dst[at, m * L : (m + 1) * L] = pbuf[pl.ds(2 * m + h, T, stride=4), :].astype(jnp.bfloat16)
-
-        loop(rows // T, body)
+            b = pl.multiple_of(c * C, C)
+            for v in range(0, C, T):
+
+                def one(u):
+                    pbuf[pl.ds(4 * (v + u), 4), :] = rec[send[0, src_row + b + v + u]]
+
+                unrolled(T, one)
+                at = pl.ds(pl.multiple_of(src_row + b, C) + v, T)
+                for h, dst in enumerate((to1, to2)):
+                    for m in range(2):
+                        x = pbuf[pl.ds(4 * v + 2 * m + h, T, stride=4), :]
+                        dst[at, m * L : (m + 1) * L] = x.astype(jnp.bfloat16)
+
+        loop(rows // C, body)
 
     def send_slopes(e, j):
         pack_slopes(block_row(e, j), s1, s2)
@@ -235,27 +252,18 @@
     pack_slopes(block_row(1, k), r1, r2)
 
     def margin(p, arrived):
-        def spread(c):
-            b = pl.multiple_of(c * T, T)
-            x = arrived[pl.ds(b, T), :].astype(jnp.float32)
-            for h in range(2):
-                pbuf[pl.ds(h, T, stride=2), :] = x[:, h * L : (h + 1) * L]
-
-            def one(u):
-                mtab[b + u] = pbuf[pl.ds(2 * u, 2), :]
-
-            unrolled(T, one)
-
-        loop(arrived.shape[0] // T, spread)
+        loop(arrived.shape[0] // C, lambda c: spread(arrived, pl.multiple_of(c * C, C), mtab, 0))
 
         def split(weight):
             high = weight.astype(jnp.bfloat16)
             low = (weight - high.astype(jnp.float32)).astype(jnp.bfloat16)
             return jnp.concatenate([high, low], axis=0)
 
-        def body(n):
+        def tile_sums(n, v):
+            base = 2 * margins * v
+
             def one(u):
-                gbuf[pl.ds(2 * u, 2), :] = mtab[slot[n * margins + u]]
+                gbuf[pl.ds(base + 2 * u, 2), :] = mtab[slot[n, u]]
 
             unrolled(margins, one)
             tile = pl.ds(n, 1)
@@ -264,7 +272,7 @@
             hit = lax.broadcasted_iota(jnp.int32, (TT, margins), 0) == cell[tile, :]
             w = jnp.where(hit, w, 0.0)
             total = jnp.sum(w, axis=1, keepdims=True)
-            parts = [gbuf[pl.ds(h, margins, stride=2), :].astype(jnp.bfloat16) for h in range(2)]
+            parts = [gbuf[pl.ds(base + h, margins, stride=2), :].astype(jnp.bfloat16) for h in range(2)]
             at = pl.ds(pl.multiple_of(n * TT, TT), TT)
             if p == 0:
                 acc = jnp.dot(split(w), jnp.concatenate(parts, axis=1), preferred_element_type=jnp.float32)
@@ -275,7 +283,11 @@
                 lanes = slice((p - 1) * L, p * L)
                 out[at, lanes] = out[at, lanes] + (acc[:TT] + acc[TT:]) / total
 
-        loop(tile_count, body)
+        def body(c):
+            for v in range(G):
+                tile_sums(c * G + v, v)
+
+        loop(tile_count // G, body)
 
     receive(0, s0, r0)
     margin(0, r0)
@@ -309,7 +321,7 @@
     hs = halo_rows.shape[1]
     rows = send_rows.shape[1]
     tile_count, margins = margin_slot.shape
-    geom = jnp.concatenate([grad_weights.reshape(12, cells), face_offsets.reshape(12, cells)], axis=0).T
+    group = 4 if tile_count % 4 == 0 else 1
     vmem = pl.BlockSpec(memory_space=pltpu.VMEM)
     smem = pl.BlockSpec(memory_space=pltpu.SMEM)
     block = pltpu.VMEM((rows, width), jnp.bfloat16)
@@ -317,13 +329,13 @@
     return pl.pallas_call(
         functools.partial(remap_kernel, regions, tiles),
         out_shape=jax.ShapeDtypeStruct((tile_count * TT, width), jnp.float32),
-        in_specs=[vmem, vmem, smem, smem, smem, smem, vmem, smem, vmem, vmem],
+        in_specs=[vmem, vmem, vmem, smem, smem, smem, smem, vmem, smem, vmem, vmem],
         out_specs=vmem,
         scratch_shapes=[
             pltpu.VMEM((cells + 2 * hs, 2, L), jnp.float32),
             pltpu.VMEM((2 * 6 * 32, L), jnp.float32),
             pltpu.VMEM((cells, 4, L), jnp.float32),
-            pltpu.VMEM((4 * 32, L), jnp.float32),
+            pltpu.VMEM((4 * 128, L), jnp.float32),
             halo,
             halo,
             block,
@@ -333,7 +345,9 @@
             block,
             block,
             pltpu.VMEM((rows, 2, L), jnp.float32),
-            pltpu.VMEM((2 * margins, L), jnp.float32),
+            pltpu.VMEM((2 * margins * group, L), jnp.float32),
+            pltpu.VMEM((32, 128), jnp.float32),
+            pltpu.VMEM((128, 32), jnp.float32),
             pltpu.SemaphoreType.DMA((2,)),
             pltpu.SemaphoreType.DMA((2,)),
             pltpu.SemaphoreType.DMA((9 * tiles,)),
@@ -343,11 +357,12 @@
         name="remap",
     )(
         values,
-        geom,
-        neighbors.reshape(-1),
-        send_rows.reshape(-1),
-        halo_rows.reshape(-1),
-        margin_slot.reshape(-1),
+        grad_weights,
+        face_offsets,
+        neighbors,
+        send_rows,
+        halo_rows,
+        margin_slot,
         margin_cell,
         margin_count,
         margin_area,

time: 210 us -> 210 us (level)
  Pallas kernels: 196 us -> 200 us
  local copies, waits for them, and re-layouts: 11.4 us -> 7.95 us
    pallas_call x1, Pallas kernels: 196 us -> 200 us  [local(): pl.pallas_call(functools.partial(remap_kernel, regions, tiles), out_shape...]
    unnamed x4 -> x3, local copies, waits for them, and re-layouts: 7.82 us -> 7.95 us
where the time goes in v3:
time: 210 us; the launch traced here: 208 us
  Pallas kernels  200 us (95%)
  local copies, waits for them, and re-layouts  7.95 us (4%)
    pallas_call x1, Pallas kernels, local(): pl.pallas_call(functools.partial(remap_kernel, regions, tiles), out_shape...  200 us
    unnamed x3, local copies, waits for them, and re-layouts  7.95 us

profile of v3, /device:TPU:0, one launch (start us, length us, event | category | flops | bytes accessed | tf_op | source)
XLA Modules:
  0.0 207.8 jit_solution(13441139673595848819)
XLA Ops:
  0.0 1.7 copy.12.weights
  1.8 1.7 copy.13.faces
  3.5 199.8 %remap.1 = f32[4096,256]{1,0:T(8,128)} custom-call(bf16[4096,256]{1,0:T(8,128)(2,1)} %vals.1, f32[2,6,4096]{2,1,0:T(8,128)} %copy.12.weights, f32[2,6,4096]{2,1,0:T(8,128)} %copy.13.faces, s32[6,4096]{1,0:T(8,128)} %nb.1, s32[1,6144]{1,0:T(1,128)} %send.1, s32[2,256]{1,0:T(2,128)} %listed.1, s32[128,128]{1,0:T(8,128)} %slot.1, s32[128,128]{1,0:T(8,128)} %cell.1, ...), custom_call_target="tpu_custom_call" | custom-call | tf_op jit(solution)/shard_map/remap/pallas_call | solution.py:329
  203.3 4.5 %copy.15 = f32[4096,256]{1,0:T(8,128)} copy(f32[4096,256]{1,0:T(8,128)} %remap.1) | data formatting | bytes 8388608
